TPU v7x, 512 devices: a whole 4x4x16 slice. The times are simulated.
512 devices in a mesh: src: 16 (over z_hi, x), tile: 32 (over y, z_lo, core).
Axes of the slice: x: 4, y: 4, z: 16 (z_hi: 4, z_lo: 4; z = z_hi * 4 + z_lo), core: 2. Of those that a mesh axis runs over, the one named last changes fastest.
Arguments:
- rhs: bfloat16 [4, 1024, 4096], P(None, 'tile', 'src'), may hold values from -6 to 6
- lower_blocks: bfloat16 [6, 1024, 1024], P(None, 'tile'), may hold values from -0.0625 to 0.0625
- dinv: bfloat16 [4, 1024, 1024], P(None, 'tile'), as said below
- adjoint_field: bfloat16 [4096, 4096], P('tile', 'src'), may hold values from -6 to 6
- side_field: bfloat16 [2, 4096, 4096], P(None, 'tile', 'src'), may hold values from -6 to 6
- stencil_coef: float32 [27, 4096], replicated, may hold values from -2 to 2
- cell_row: int32 [4096], replicated, may hold values from 0 to 4095, each once
Outputs:
- wavefield: bfloat16 [4, 1024, 4096], P(None, 'tile', 'src')
- gradient: float32 [4096], P('tile')
Inputs may be any that keep to these rules, and one draw needn't show every extreme that they name: Each block of dinv is lower triangular with a diagonal between 0.6 and 1.6.
All inputs are finite; a program needn't handle non-finite values.
Results may differ from a plain program's by a relative error of at most 0.025.
Values may be sent and summed in bfloat16 or wider, within the bound.
A program may use at most 64 MiB of HBM per device.

v0:
```python
import math

import jax
import jax.numpy as jnp
from jax import lax
from jax.sharding import PartitionSpec as P

GZ = 64


def with_halo(cells, sides, width):
    for axis, dim in sides:
        count = lax.axis_size(axis)
        ends = count - 1
        head = lax.slice_in_dim(cells, 0, width, axis=dim)
        tail = lax.slice_in_dim(cells, cells.shape[dim] - width, cells.shape[dim], axis=dim)
        cells = jnp.concatenate(
            [
                lax.ppermute(tail, axis, [(i, (i + 1) % count) for i in range(ends)]),
                cells,
                lax.ppermute(head, axis, [((i + 1) % count, i) for i in range(ends)]),
            ],
            axis=dim,
        )
    return cells


def shards(rhs, lower_blocks, dinv, adjoint_field, side_field, stencil_coef, cell_row):
    my_tile = lax.axis_index("tile")
    panels = rhs.shape[0]
    part_rows = rhs.shape[1]
    sources = rhs.shape[2]
    solved_full = []
    solved_rows = []
    for target in range(panels):
        running = rhs[target].astype(jnp.float32)
        for earlier in range(target):
            running = running - jnp.dot(
                lower_blocks[target * (target - 1) // 2 + earlier],
                solved_full[earlier],
                preferred_element_type=jnp.float32,
            )
        residual = running.astype(jnp.bfloat16)

        def absorb(carried, shard_rows, offset, inverse=dinv[target]):
            return jnp.dot(inverse, shard_rows, preferred_element_type=jnp.float32)

        start = jnp.zeros((part_rows, sources), jnp.float32)
        panel_rows = absorb(
            start, lax.all_gather(residual, "tile", axis=0, tiled=True), jnp.int32(0)
        ).astype(jnp.bfloat16)
        solved_rows.append(panel_rows)
        if target + 1 < panels:
            solved_full.append(lax.all_gather(panel_rows, "tile", axis=0, tiled=True))
    adjoint_rows = [None] * panels
    for target in reversed(range(panels)):
        if target == panels - 1:
            wave = solved_rows[target]
        else:

            def coupling(offset, count, target=target, known=tuple(adjoint_rows)):
                running = jnp.zeros((count, sources), jnp.float32)
                for later in range(target + 1, panels):
                    block = lower_blocks[later * (later - 1) // 2 + target]
                    running = running + jnp.einsum(
                        "mc,ms->cs", block, known[later], preferred_element_type=jnp.float32
                    )
                return running

            summed = lax.psum_scatter(
                coupling(jnp.int32(0), part_rows * lax.axis_size("tile")).astype(jnp.bfloat16),
                "tile",
                scatter_dimension=0,
                tiled=True,
            ).astype(jnp.float32)
            wave = (solved_rows[target].astype(jnp.float32) - summed).astype(jnp.bfloat16)

        def diagonal(offset, count, target=target, wave=wave):
            columns = dinv[target]
            return jnp.einsum("mc,ms->cs", columns, wave, preferred_element_type=jnp.float32)

        adjoint_rows[target] = lax.psum_scatter(
            diagonal(jnp.int32(0), part_rows * lax.axis_size("tile")).astype(jnp.bfloat16),
            "tile",
            scatter_dimension=0,
            tiled=True,
        )
    wavefield = jnp.stack(adjoint_rows)
    slab = adjoint_field.shape[0]
    gathered = lax.all_gather(wavefield, "tile", axis=1, tiled=True).reshape(-1, sources)
    ordered = jnp.take(gathered, cell_row, axis=0)
    margin = GZ + 1
    whole = jnp.pad(ordered, ((margin, margin), (0, 0)))
    middle = lax.dynamic_slice_in_dim(whole, my_tile * slab, slab + 2 * margin, 0)
    sides = with_halo(side_field, (("tile", 1),), GZ)
    sides = jnp.pad(sides, ((0, 0), (1, 1), (0, 0)))
    planes = (sides[0], middle, sides[1])
    local_coef = lax.dynamic_slice_in_dim(stencil_coef, my_tile * slab, slab, 1)
    zpos = jnp.arange(slab) % GZ
    field = jnp.zeros((slab, sources), jnp.float32)
    for offset_x in (-1, 0, 1):
        plane = planes[offset_x + 1]
        for offset_y in (-1, 0, 1):
            for offset_z in (-1, 0, 1):
                number = (offset_x + 1) * 9 + (offset_y + 1) * 3 + (offset_z + 1)
                begin = margin + offset_y * GZ + offset_z
                near = plane[begin : begin + slab]
                weight_row = local_coef[number]
                if offset_z == -1:
                    weight_row = jnp.where(zpos > 0, weight_row, 0.0)
                if offset_z == 1:
                    weight_row = jnp.where(zpos < GZ - 1, weight_row, 0.0)
                field = field + weight_row[:, None] * near.astype(jnp.float32)
    partial_sum = jnp.sum(adjoint_field.astype(jnp.float32) * field, axis=1)
    total = lax.psum(partial_sum, "src")
    gradient = total * (1.0 / math.sqrt(sources * lax.axis_size("src")))
    return (wavefield, gradient)


def solution(mesh):
    in_specs = (
        P(None, "tile", "src"),
        P(None, "tile", None),
        P(None, "tile", None),
        P("tile", "src"),
        P(None, "tile", "src"),
        P(),
        P(),
    )
    out_specs = (P(None, "tile", "src"), P("tile"))
    return jax.shard_map(shards, mesh=mesh, in_specs=in_specs, out_specs=out_specs, check_vma=False)
```

profile of v0, /device:TPU:1, one launch (start us, length us, event | category | flops | bytes accessed | tf_op | source)
XLA Modules:
  0.0 1484.1 jit_solution(10237986665572901675)
XLA Ops:
  7.2 0.8 slice.287
  8.1 48.1 %all-gather = bf16[1,1024,256]{2,1,0:T(8,128)(2,1)S(1)} all-gather(bf16[1,32,256]{2,1,0:T(8,128)(2,1)S(1)} %slice.287), channel_id=2, replica_groups=mesh['src'=16,'tile'=32] {'tile'}, dimensions={1}, use_global_device_ids=true | all-gather | bytes 540672 | tf_op jit(solution)/shard_map/all_gather | solution.py:50
  56.1 1.0 convolution_convert_fusion.8
  57.2 40.0 %all_gather.25 = bf16[1024,256]{1,0:T(8,128)(2,1)S(1)} all-gather(bf16[32,256]{1,0:T(8,128)(2,1)S(1)} %convolution_convert_fusion.8), channel_id=1, replica_groups=mesh['src'=16,'tile'=32] {'tile'}, dimensions={0}, use_global_device_ids=true | all-gather | bytes 540672 | tf_op jit(solution)/shard_map/all_gather | solution.py:54
  97.2 1.0 fusion.11
  98.5 0.2 fusion.13
  98.7 41.3 %all_gather.26 = bf16[1024,256]{1,0:T(8,128)(2,1)S(1)} all-gather(bf16[32,256]{1,0:T(8,128)(2,1)S(1)} %fusion.15), channel_id=1, replica_groups=mesh['src'=16,'tile'=32] {'tile'}, dimensions={0}, use_global_device_ids=true | all-gather | bytes 540672 | tf_op jit(solution)/shard_map/all_gather | solution.py:50
  140.2 40.0 %all_gather.27 = bf16[1024,256]{1,0:T(8,128)(2,1)S(1)} all-gather(bf16[32,256]{1,0:T(8,128)(2,1)S(1)} %fusion.18), channel_id=1, replica_groups=mesh['src'=16,'tile'=32] {'tile'}, dimensions={0}, use_global_device_ids=true | all-gather | bytes 540672 | tf_op jit(solution)/shard_map/all_gather | solution.py:54
  180.4 0.2 fusion.16
  180.6 41.3 %all_gather.28 = bf16[1024,256]{1,0:T(8,128)(2,1)S(1)} all-gather(bf16[32,256]{1,0:T(8,128)(2,1)S(1)} %fusion.16), channel_id=1, replica_groups=mesh['src'=16,'tile'=32] {'tile'}, dimensions={0}, use_global_device_ids=true | all-gather | bytes 540672 | tf_op jit(solution)/shard_map/all_gather | solution.py:50
  222.1 40.1 %all_gather.29 = bf16[1024,256]{1,0:T(8,128)(2,1)S(1)} all-gather(bf16[32,256]{1,0:T(8,128)(2,1)S(1)} %fusion.19), channel_id=1, replica_groups=mesh['src'=16,'tile'=32] {'tile'}, dimensions={0}, use_global_device_ids=true | all-gather | bytes 540672 | tf_op jit(solution)/shard_map/all_gather | solution.py:54
  262.4 41.3 %all_gather.30 = bf16[1024,256]{1,0:T(8,128)(2,1)S(1)} all-gather(bf16[32,256]{1,0:T(8,128)(2,1)S(1)} %fusion.17), channel_id=1, replica_groups=mesh['src'=16,'tile'=32] {'tile'}, dimensions={0}, use_global_device_ids=true | all-gather | bytes 540672 | tf_op jit(solution)/shard_map/all_gather | solution.py:50
  303.7 0.6 fusion.2
  304.3 1.0 copy.39
  305.4 143.6 %reduce-scatter.22.cloned.1.call-done = bf16[32,256]{1,0:T(8,128)(2,1)} async-done(((bf16[1024,256]{1,0:T(8,128)(2,1)}), bf16[32,256]{1,0:T(8,128)(2,1)}) %reduce-scatter.22.cloned.1.call-update) | async-done | bytes 16400
  449.0 1.9 fusion.3
  451.0 146.6 %reduce-scatter.16.cloned.1.call-done = bf16[32,256]{1,0:T(8,128)(2,1)} async-done(((bf16[1024,256]{1,0:T(8,128)(2,1)}), bf16[32,256]{1,0:T(8,128)(2,1)}) %reduce-scatter.16.cloned.1.call-update) | async-done | bytes 16400 | tf_op jit(solution)/shard_map/reduce_scatter | solution.py:70
  597.7 1.0 fusion.4
  598.7 1.0 copy.41
  599.8 146.4 %reduce-scatter.24.cloned.1.call-done = bf16[32,256]{1,0:T(8,128)(2,1)} async-done(((bf16[1024,256]{1,0:T(8,128)(2,1)}), bf16[32,256]{1,0:T(8,128)(2,1)}) %reduce-scatter.24.cloned.1.call-update) | async-done | bytes 16400
  746.2 1.1 fusion.65
  747.3 1.1 fusion.8
  748.5 146.1 %reduce-scatter.18.cloned.1.call-done = bf16[32,256]{1,0:T(8,128)(2,1)} async-done(((bf16[1024,256]{1,0:T(8,128)(2,1)}), bf16[32,256]{1,0:T(8,128)(2,1)}) %reduce-scatter.18.cloned.1.call-update) | async-done | bytes 16400 | tf_op jit(solution)/shard_map/reduce_scatter | solution.py:70
  894.6 1.0 fusion.5
  895.7 1.0 copy.43
  896.7 146.2 %reduce-scatter.26.cloned.1.call-done = bf16[32,256]{1,0:T(8,128)(2,1)} async-done(((bf16[1024,256]{1,0:T(8,128)(2,1)}), bf16[32,256]{1,0:T(8,128)(2,1)}) %reduce-scatter.26.cloned.1.call-update) | async-done | bytes 16400
  1042.9 1.1 fusion.72
  1044.0 0.3 convolution_add_fusion.1
  1044.3 1.2 fusion.7
  1045.6 145.8 %reduce-scatter.20.cloned.1.call-done = bf16[32,256]{1,0:T(8,128)(2,1)} async-done(((bf16[1024,256]{1,0:T(8,128)(2,1)}), bf16[32,256]{1,0:T(8,128)(2,1)}) %reduce-scatter.20.cloned.1.call-update) | async-done | bytes 16400 | tf_op jit(solution)/shard_map/reduce_scatter | solution.py:70
  1191.4 1.0 fusion.6
  1192.5 1.0 copy.45
  1193.9 145.9 %reduce-scatter.28.cloned.1.call-done = bf16[32,256]{1,0:T(8,128)(2,1)} async-done(((bf16[1024,256]{1,0:T(8,128)(2,1)}), bf16[32,256]{1,0:T(8,128)(2,1)}) %reduce-scatter.28.cloned.1.call-update) | async-done | bytes 16400
  1339.8 0.8 copy.46
  1340.8 0.8 copy.30
  1341.6 7.2 collective-permute-start.1
  1348.7 1.9 collective-permute-start
  1350.7 0.9 dynamic-slice_bitcast_fusion.25
  1351.6 1.1 fusion.99
  1352.8 0.8 fusion.100
  1353.7 0.8 copy.32
  1354.5 54.1 %all-gather.3.cloned.1.call-done = bf16[4,1024,256]{2,0,1:T(4,128)(2,1)} async-done(((bf16[4,32,256]{2,0,1:T(4,128)(2,1)}), bf16[4,1024,256]{2,0,1:T(4,128)(2,1)}) %all-gather.3.cloned.1.call-update) | async-done | bytes 2097168 | tf_op jit(solution)/shard_map/all_gather | solution.py:90
  1408.6 1.9 copy.31
  1410.5 17.0 %gather_fusion = bf16[4096,256]{1,0:T(8,128)(2,1)} fusion(bf16[4096,256]{1,0:T(8,128)(2,1)S(1)} %bitcast.309, s32[4096]{0:T(1024)S(1)} %fusion.97), kind=kCustom, calls=%fused_computation | custom fusion | bytes 4210688 | tf_op jit(solution)/shard_map/jit(_take)/gather | solution.py:91
  1427.5 2.0 broadcast_select_fusion
  1429.5 1.0 fusion.29
  1430.5 46.2 %psum.7 = f32[128]{0:T(128)S(1)} all-reduce(f32[128]{0:T(128)S(1)} %fusion.29), channel_id=1, replica_groups=mesh['src'=16,'tile'=32] {'src'}, use_global_device_ids=true, to_apply=%region_8.9 | all-reduce | flops 128 | bytes 1024 | tf_op jit(solution)/shard_map/psum | solution.py:115
  1476.7 0.5 broadcast_multiply_fusion
  (52 shorter events, 2.0 us)
Async XLA Ops:
  7.2 91.1 %copy-start.7 = (bf16[4,32,256]{2,1,0:T(8,128)(2,1)S(1)}, bf16[4,32,256]{2,1,0:T(8,128)(2,1)}, u32[]{:S(2)}) copy-start(bf16[4,32,256]{2,1,0:T(8,128)(2,1)} %param.7) | copy-start | bytes 196612
  7.2 132.8 %copy-start.2 = (bf16[4,32,1024]{2,1,0:T(8,128)(2,1)S(1)}, bf16[4,32,1024]{2,1,0:T(8,128)(2,1)}, u32[]{:S(2)}) copy-start(bf16[4,32,1024]{2,1,0:T(8,128)(2,1)} %param.9) | copy-start | bytes 786436
  7.2 91.1 %copy-start.1 = (bf16[6,32,1024]{2,1,0:T(8,128)(2,1)S(1)}, bf16[6,32,1024]{2,1,0:T(8,128)(2,1)}, u32[]{:S(2)}) copy-start(bf16[6,32,1024]{2,1,0:T(8,128)(2,1)} %param.8) | copy-start | bytes 1179652
  7.2 441.8 %reduce-scatter.22.cloned.1.call-start = ((), (), s32[]{:S(2)}) async-start(), calls=%async_computation.11 | async-start | bytes 540672
  305.4 292.3 %reduce-scatter.16.cloned.1.call-start = ((), (), s32[]{:S(2)}) async-start(), calls=%async_computation.7 | async-start | bytes 540672 | tf_op jit(solution)/shard_map/reduce_scatter | solution.py:70
  449.0 298.3 %copy-start.3 = (bf16[32,256]{1,0:T(8,128)(2,1)S(1)}, bf16[32,256]{1,0:T(8,128)(2,1)}, u32[]{:S(2)}) copy-start(bf16[32,256]{1,0:T(8,128)(2,1)} %reduce-scatter.22.cloned.1.call-done) | copy-start | bytes 49156
  451.0 295.2 %reduce-scatter.24.cloned.1.call-start = ((), (), s32[]{:S(2)}) async-start(), calls=%async_computation.12 | async-start | bytes 540672
  599.8 294.9 %reduce-scatter.18.cloned.1.call-start = ((), (), s32[]{:S(2)}) async-start(), calls=%async_computation.8 | async-start | bytes 540672 | tf_op jit(solution)/shard_map/reduce_scatter | solution.py:70
  748.4 295.5 %copy-start.4 = (bf16[32,256]{1,0:T(8,128)(2,1)S(1)}, bf16[32,256]{1,0:T(8,128)(2,1)}, u32[]{:S(2)}) copy-start(bf16[32,256]{1,0:T(8,128)(2,1)} %reduce-scatter.24.cloned.1.call-done) | copy-start | bytes 49156
  748.5 294.5 %reduce-scatter.26.cloned.1.call-start = ((), (), s32[]{:S(2)}) async-start(), calls=%async_computation.13 | async-start | bytes 540672
  896.7 294.7 %reduce-scatter.20.cloned.1.call-start = ((), (), s32[]{:S(2)}) async-start(), calls=%async_computation.9 | async-start | bytes 540672 | tf_op jit(solution)/shard_map/reduce_scatter | solution.py:70
  1044.3 149.4 %copy-start.5 = (bf16[32,256]{1,0:T(8,128)(2,1)S(1)}, bf16[32,256]{1,0:T(8,128)(2,1)}, u32[]{:S(2)}) copy-start(bf16[32,256]{1,0:T(8,128)(2,1)} %reduce-scatter.26.cloned.1.call-done) | copy-start | bytes 49156
  1045.5 296.0 %copy-start = (bf16[2,128,256]{2,1,0:T(8,128)(2,1)S(1)}, bf16[2,128,256]{2,1,0:T(8,128)(2,1)}, u32[]{:S(2)}) copy-start(bf16[2,128,256]{2,1,0:T(8,128)(2,1)} %param.11) | copy-start | bytes 393220
  1045.5 307.2 %copy-start.8 = (s32[4096]{0:T(1024)S(1)}, s32[4096]{0:T(1024)}, u32[]{:S(2)}) copy-start(s32[4096]{0:T(1024)} %param.13) | copy-start | bytes 49156
  1045.5 294.3 %reduce-scatter.28.cloned.1.call-start = ((), (), s32[]{:S(2)}) async-start(), calls=%async_computation.14 | async-start | bytes 540672
  1193.5 215.1 %all-gather.3.cloned.1.call-start = ((), (), s32[]{:S(2)}) async-start(), calls=%async_computation.10 | async-start | bytes 2162688 | tf_op jit(solution)/shard_map/all_gather | solution.py:90
  1341.6 12.0 collective-permute-start.1
  1348.7 4.8 collective-permute-start
  1427.5 2.0 copy-start.6
Sparse Core Ops, SparseCore 0:
  305.5 143.4 reduce-scatter.21
  452.0 145.6 reduce-scatter.15
  600.5 145.7 reduce-scatter.23
  749.1 145.4 reduce-scatter.17
  897.2 145.6 reduce-scatter.25
  1045.8 145.5 reduce-scatter.19
  1194.2 145.6 reduce-scatter.27
  1342.2 66.3 all-gather.2
where the time goes:
time: 1490 us; the launch traced here: 1480 us
  waiting for transfers between devices  1070 us (72%)
  blocking collectives  338 us (23%)
  local copies, waits for them, and re-layouts  27.5 us (2%)
    unnamed x12, waiting for transfers between devices  582 us
    reduce_scatter x3, waiting for transfers between devices, shards(): lax.psum_scatter(coupling(jnp.int32(0), part_rows * lax.axis_size('tile')...  439 us
    all_gather x4, blocking collectives, shards(): lax.all_gather(residual, 'tile', axis=0, tiled=True)  172 us
    all_gather x3, blocking collectives, shards(): solved_full.append(lax.all_gather(panel_rows, 'tile', axis=0, tiled=True))  120 us
    all_gather x1, waiting for transfers between devices, shards(): lax.all_gather(wavefield, 'tile', axis=1, tiled=True).reshape(-1, sources)  54.1 us
    psum x1, blocking collectives, shards(): total = lax.psum(partial_sum, 'src')  46.2 us
  transfers between devices with their start and end apart: 10, of which 8 were waited for; matrix products, arithmetic and copies ran while one was open for 0% of the time, Pallas kernels for 0%

commit v1 on v0

v1 whole, which is shorter than its diff:
```python
import functools

import jax
import jax.numpy as jnp
from jax import lax
from jax.experimental import pallas as pl
from jax.experimental.pallas import tpu as pltpu
from jax.sharding import PartitionSpec as P

MESH = pl.DeviceIdType.MESH
F32 = jnp.float32
BF16 = jnp.bfloat16
NY = 4
NC = 8
PANELS = 4
PART = 32
SRC = 32
QUARTER = 256
PW = 1024
WIDE = 1280
NN = (((1,), (0,)), ((), ()))
NT = (((1,), (1,)), ((), ()))

ORDER = [("d", 0), ("l", 0), ("d", 1), ("l", 1), ("l", 2), ("d", 2), ("l", 3), ("l", 4), ("l", 5), ("d", 3)]
PLACE = {unit: number for number, unit in enumerate(ORDER)}


def block_of(later, earlier):
    return later * (later - 1) // 2 + earlier


def dot(a, b, dims):
    return lax.dot_general(a, b, dims, preferred_element_type=F32)


def kernel(
    rhs, lower, dinv, adj, side, coef, cells,
    wave_out, grad_out,
    dcols, lrows, x_send, x_got, s_send, s_got, halo, order, perm, acc,
    part_send, part_got, y_full, z_own, z_all, grid, field, w_send, w_got,
    g1_send, g1_got, g2_send, g2_got,
    dy_s, dy_r, xa_s, xa_r, sa_s, sa_r, mz_s, mz_r, mc_s, mc_r, st_s, st_r,
    za_s, za_r, ha_s, ha_r, wf_s, wf_r, g1_s, g1_r, g2_s, g2_r,
):
    s = lax.axis_index("src")
    t = lax.axis_index("tile")
    x, zh = lax.rem(s, 4), lax.div(s, 4)
    y, zc = lax.div(t, NC), lax.rem(t, NC)
    zl, core = lax.div(zc, 2), lax.rem(zc, 2)
    z = zh * 4 + zl

    def dev(x, y, z, c):
        return (lax.div(z, 4) * 4 + x, (y * 4 + lax.rem(z, 4)) * 2 + c)

    def y_peer(d):
        return dev(x, lax.rem(y + d, NY), z, core)

    def z_peer(d):
        return dev(x, y, lax.rem(z + d + 16, 16), core)

    def c_index(d):
        return lax.rem(zc + d, NC)

    def c_peer(d):
        return (s, y * NC + c_index(d))

    def s_peer(d):
        return (lax.rem(s + d, 16), t)

    sibling = dev(x, y, z, 1 - core)
    started = []

    def send(src, dst, send_sem, recv_sem, device):
        copy = pltpu.make_async_remote_copy(
            src_ref=src, dst_ref=dst, send_sem=send_sem, recv_sem=recv_sem,
            device_id=device, device_id_type=MESH,
        )
        copy.start()
        started.append(copy)
        return copy

    barrier = pltpu.get_barrier_semaphore()
    peers = [y_peer(d) for d in (1, 2, 3)] + [c_peer(d) for d in range(1, NC)]
    peers += [z_peer(d) for d in (1, -1, 2, -2)] + [s_peer(d) for d in range(1, 16)]
    for peer in peers:
        pl.semaphore_signal(barrier, inc=1, device_id=peer, device_id_type=MESH)

    x_send[...] = rhs[...].astype(F32).reshape(PANELS * PART, 256).T.astype(BF16)
    own_cols = pl.ds(pl.multiple_of(y * QUARTER, QUARTER), QUARTER)
    for j in range(PANELS):
        dcols[j, y, zc] = dinv[j, :, own_cols]
    for b in range(6):
        lrows[b, zc] = lower[b]
    own_rows = pl.ds(pl.multiple_of(zc * SRC, SRC), SRC)
    x_got[zc] = x_send[own_rows, :]
    pl.semaphore_wait(barrier, len(peers))

    dy = []
    for j in range(PANELS):
        row = []
        for d in (1, 2, 3):
            cols = pl.ds(pl.multiple_of(lax.rem(y + d, NY) * QUARTER, QUARTER), QUARTER)
            row.append(send(dinv.at[j, :, cols], dcols.at[j, y, zc], dy_s.at[j, d - 1], dy_r.at[j, d - 1], y_peer(d)))
        dy.append(row)
        if j == 0:
            xa = []
            for d in range(1, NC):
                part = pl.ds(pl.multiple_of(c_index(d) * SRC, SRC), SRC)
                xa.append(send(x_send.at[part, :], x_got.at[zc], xa_s.at[d - 1], xa_r.at[d - 1], c_peer(d)))

    def unit_ref(unit, slot):
        kind, number = unit
        return dcols.at[number, :, slot] if kind == "d" else lrows.at[number, slot]

    def slot_at(d):
        return lax.rem(zl + d, 4) * 2 + core

    mz = {}
    mc = {}

    def push(unit):
        n = PLACE[unit]
        if unit[0] == "d":
            for copy in dy[unit[1]]:
                copy.wait_recv()
        mine = unit_ref(unit, zc)
        far = 2 - 4 * lax.rem(core + n, 2)
        mz[unit] = [
            send(mine, mine, mz_s.at[n, k], mz_r.at[n, k], z_peer(d)) for k, d in enumerate((1, -1, far))
        ]
        mc[unit] = [send(mine, mine, mc_s.at[n, 0], mc_r.at[n, 0], sibling)]

    def pump(unit):
        n = PLACE[unit]
        for k, d in enumerate((3, 1, 2)):
            mz[unit][k].wait_recv()
            here = unit_ref(unit, slot_at(d))
            mc[unit].append(send(here, here, mc_s.at[n, k + 1], mc_r.at[n, k + 1], sibling))

    def ready(unit):
        for copy in mc[unit]:
            copy.wait_recv()

    push(("l", 0))
    for unit in ORDER:
        if unit != ("l", 0):
            push(unit)

    s_send[:, 0:128] = adj[...].astype(F32).T.astype(BF16)
    s_send[:, 128:256] = side[0].astype(F32).T.astype(BF16)
    s_send[:, 256:384] = side[1].astype(F32).T.astype(BF16)
    s_got[zc] = s_send[own_rows, :]
    sa = []
    for d in range(1, NC):
        part = pl.ds(pl.multiple_of(c_index(d) * SRC, SRC), SRC)
        sa.append(send(s_send.at[part, :], s_got.at[zc], sa_s.at[d - 1], sa_r.at[d - 1], c_peer(d)))

    lane = lax.broadcasted_iota(jnp.int32, (SRC, 128), 1)
    for copy in xa:
        copy.wait_recv()
    for p in range(PANELS):
        for half in range(2):
            block = jnp.zeros((SRC, 128), F32)
            for q in range(4):
                piece = pltpu.roll(x_got[half * 4 + q].astype(F32), ((q - p) * PART) % 128, 1)
                block = jnp.where(lane // PART == q, piece, block)
            acc[p, :, half * 128:(half + 1) * 128] = block

    order[0:8, :] = cells[pl.ds(pl.multiple_of(lax.rem(y + 3, NY) * 8, 8), 8), :]
    left = jnp.where(y == 0, -1, order[7:8, :])
    order[8:16, :] = cells[pl.ds(pl.multiple_of(lax.rem(y + 1, NY) * 8, 8), 8), :]
    right = jnp.where(y == NY - 1, -1, order[8:9, :])
    middle = cells[pl.ds(pl.multiple_of(y * 8, 8), 8), :]
    wanted = [left] + [middle[i:i + 1, :] for i in range(8)] + [right]

    def fill(i, carry):
        rows = lax.broadcasted_iota(jnp.int32, (QUARTER, 128), 0) + i * QUARTER
        at = pl.ds(pl.multiple_of(i * QUARTER, QUARTER), QUARTER)
        for n, row in enumerate(wanted):
            hit = jnp.where(rows == row, 1.0, 0.0).astype(BF16)
            perm[at, n * 128:(n + 1) * 128] = hit
        return carry

    lax.fori_loop(0, 16, fill, 0)

    def share(step, value):
        part_send[step] = value.astype(BF16)
        return [
            send(part_send.at[step], part_got.at[step, d - 1], st_s.at[step, d - 1], st_r.at[step, d - 1], y_peer(d))
            for d in (1, 2, 3)
        ]

    def total(step, copies):
        for copy in copies:
            copy.wait_recv()
        value = part_send[step].astype(F32)
        for d in range(3):
            value = value + part_got[step, d].astype(F32)
        return value

    def d_whole(j):
        return dcols[j].reshape(PW, QUARTER)

    def l_whole(later, earlier):
        return lrows[block_of(later, earlier)].reshape(QUARTER, PW)

    pump(("d", 0))
    pump(("l", 0))
    ready(("d", 0))
    windows = {
        0: [("d", 1), ("l", 1)],
        1: [("l", 2), ("d", 2), ("l", 3)],
        2: [("l", 4), ("l", 5), ("d", 3)],
        3: [],
    }
    for j in range(PANELS):
        resid = acc[j].astype(BF16)
        copies = share(j, dot(resid, d_whole(j), NT))
        for unit in windows[j]:
            pump(unit)
        if j + 1 < PANELS:
            for k in range(j):
                ready(("l", block_of(j + 1, k)))
                acc[j + 1] = acc[j + 1] - dot(y_full[k], l_whole(j + 1, k), NT)
            ready(("l", block_of(j + 1, j)))
            ready(("d", j + 1))
        if j == 3:
            for copy in sa:
                copy.wait_recv()
            ha = [
                send(s_got.at[7, :, pl.ds(128, 256)], halo.at[0], ha_s.at[0], ha_r.at[0], y_peer(1)),
                send(s_got.at[0, :, pl.ds(128, 256)], halo.at[1], ha_s.at[1], ha_r.at[1], y_peer(3)),
            ]
        y_full[j] = total(j, copies).astype(BF16)
        if j + 1 < PANELS:
            acc[j + 1] = acc[j + 1] - dot(y_full[j], l_whole(j + 1, j), NT)

    zpos = lax.rem(lax.broadcasted_iota(jnp.int32, (1, PW), 1), 64)
    own_cells = pl.ds(pl.multiple_of(y * PW, PW), PW)

    def stencil(plane, offset_x):
        value = jnp.zeros((SRC, PW), F32)
        for offset_y in (-1, 0, 1):
            for offset_z in (-1, 0, 1):
                number = (offset_x + 1) * 9 + (offset_y + 1) * 3 + (offset_z + 1)
                weight = coef[number:number + 1, own_cells]
                if offset_z == -1:
                    weight = jnp.where(zpos > 0, weight, 0.0)
                if offset_z == 1:
                    weight = jnp.where(zpos < 63, weight, 0.0)
                shift = offset_y * 64 + offset_z
                near = pltpu.roll(plane, (-shift) % WIDE, 1) if shift else plane
                value = value + weight * near[:, 128:128 + PW]
        return value

    def side_plane(n):
        low = 128 * (n + 1)
        first = jnp.where(y == 0, 0.0, halo[0, :, 128 * n:128 * (n + 1)].astype(F32))
        last = jnp.where(y == NY - 1, 0.0, halo[1, :, 128 * n:128 * (n + 1)].astype(F32))
        inner = [s_got[i, :, low:low + 128].astype(F32) for i in range(NC)]
        return jnp.concatenate([first] + inner + [last], axis=1)

    def order_cells(j):
        value = jnp.zeros((SRC, WIDE), F32)
        for q in range(NY):
            rows = slice((j * NY + q) * QUARTER, (j * NY + q + 1) * QUARTER)
            value = value + dot(z_all[j, q], perm[rows, :], NN)
        return value

    za = {}
    later_term = {}
    whole = y_full[3]
    for j in reversed(range(PANELS)):
        z_j = dot(whole, d_whole(j), NN).astype(BF16)
        z_own[j] = z_j
        if j > 0:
            term = dot(z_j, l_whole(j, j - 1), NN)
            if j - 1 in later_term:
                term = term + later_term[j - 1]
            copies = share(7 - j, term)
        z_all[j, y] = z_j
        za[j] = [
            send(z_own.at[j], z_all.at[j, y], za_s.at[j, d - 1], za_r.at[j, d - 1], y_peer(d)) for d in (1, 2, 3)
        ]
        if j > 0:
            for earlier in range(j - 1):
                more = dot(z_j, l_whole(j, earlier), NN)
                later_term[earlier] = later_term[earlier] + more if earlier in later_term else more
            if j == 3:
                for copy in ha:
                    copy.wait_recv()
                field[...] = stencil(side_plane(0), -1) + stencil(side_plane(1), 1)
            else:
                for copy in za[j + 1]:
                    copy.wait_recv()
                grid[...] = order_cells(j + 1) if j == 2 else grid[...] + order_cells(j + 1)
            whole = (y_full[j - 1].astype(F32) - total(7 - j, copies)).astype(BF16)

    for d in range(NC):
        pass
    z_f32 = [z_own[p].astype(F32) for p in range(PANELS)]
    for n in range(NC):
        block = jnp.zeros((SRC, 128), F32)
        for p in range(PANELS):
            piece = z_f32[p][:, (n // 4) * 128:(n // 4 + 1) * 128]
            piece = pltpu.roll(piece, ((p - n % 4) * PART) % 128, 1)
            block = jnp.where(lane // PART == p, piece, block)
        w_send[n] = block.astype(BF16)
    w_got[zc] = w_send[zc]
    wf = []
    for d in range(1, NC):
        wf.append(send(w_send.at[c_index(d)], w_got.at[zc], wf_s.at[d - 1], wf_r.at[d - 1], c_peer(d)))

    for copy in za[1]:
        copy.wait_recv()
    grid[...] = grid[...] + order_cells(1)
    for copy in za[0]:
        copy.wait_recv()
    field_all = field[...] + stencil(grid[...] + order_cells(0), 0)
    for n in range(NC):
        here = s_got[n, :, 0:128].astype(F32) * field_all[:, n * 128:(n + 1) * 128]
        g1_send[n] = jnp.sum(here, axis=0, keepdims=True)

    g1 = []
    for d in range(1, NC):
        g1.append(send(g1_send.at[c_index(d)], g1_got.at[d - 1], g1_s.at[d - 1], g1_r.at[d - 1], c_peer(d)))
    for copy in g1:
        copy.wait_recv()
    group = g1_send[zc]
    for d in range(1, NC):
        group = group + g1_got[d - 1]
    g2_send[...] = group
    g2 = []
    for d in range(1, 16):
        g2.append(send(g2_send, g2_got.at[d - 1], g2_s.at[d - 1], g2_r.at[d - 1], s_peer(d)))

    for copy in wf:
        copy.wait_recv()
    back = w_got[...].astype(F32).reshape(256, 128).T
    wave_out[...] = back.reshape(PANELS, PART, 256).astype(BF16)

    for copy in g2:
        copy.wait_recv()
    for d in range(1, 16):
        group = group + g2_got[d - 1]
    grad_out[...] = group * (1.0 / 64.0)
    for copy in started:
        copy.wait_send()


def shards(rhs, lower_blocks, dinv, adjoint_field, side_field, stencil_coef, cell_row):
    dma = pltpu.SemaphoreType.DMA
    pairs = [(4, 3), (7,), (7,), (10, 3), (10, 4), (7, 3), (4, 3), (2,), (7,), (7,), (15,)]
    wavefield, gradient = pl.pallas_call(
        kernel,
        out_shape=(
            jax.ShapeDtypeStruct((PANELS, PART, 256), BF16),
            jax.ShapeDtypeStruct((1, 128), F32),
        ),
        in_specs=[pl.BlockSpec(memory_space=pltpu.VMEM)] * 7,
        out_specs=(pl.BlockSpec(memory_space=pltpu.VMEM),) * 2,
        scratch_shapes=[
            pltpu.VMEM((PANELS, NY, NC, PART, QUARTER), BF16),
            pltpu.VMEM((6, NC, PART, PW), BF16),
            pltpu.VMEM((256, 128), BF16),
            pltpu.VMEM((NC, SRC, 128), BF16),
            pltpu.VMEM((256, 384), BF16),
            pltpu.VMEM((NC, SRC, 384), BF16),
            pltpu.VMEM((2, SRC, 256), BF16),
            pltpu.VMEM((16, 128), jnp.int32),
            pltpu.VMEM((4096, WIDE), BF16),
            pltpu.VMEM((PANELS, SRC, QUARTER), F32),
            pltpu.VMEM((7, SRC, PW), BF16),
            pltpu.VMEM((7, 3, SRC, PW), BF16),
            pltpu.VMEM((PANELS, SRC, PW), BF16),
            pltpu.VMEM((PANELS, SRC, QUARTER), BF16),
            pltpu.VMEM((PANELS, NY, SRC, QUARTER), BF16),
            pltpu.VMEM((SRC, WIDE), F32),
            pltpu.VMEM((SRC, PW), F32),
            pltpu.VMEM((NC, SRC, 128), BF16),
            pltpu.VMEM((NC, SRC, 128), BF16),
            pltpu.VMEM((NC, 1, 128), F32),
            pltpu.VMEM((NC - 1, 1, 128), F32),
            pltpu.VMEM((1, 128), F32),
            pltpu.VMEM((15, 1, 128), F32),
        ]
        + [dma(shape) for shape in pairs for _ in range(2)],
        compiler_params=pltpu.CompilerParams(
            collective_id=0, has_side_effects=True, vmem_limit_bytes=48 * 1024 * 1024
        ),
        cost_estimate=pl.CostEstimate(flops=10**9, bytes_accessed=4 * 10**6, transcendentals=0),
    )(rhs, lower_blocks, dinv, adjoint_field, side_field, stencil_coef, cell_row.reshape(32, 128))
    return wavefield, gradient.reshape(128)


def solution(mesh):
    in_specs = (
        P(None, "tile", "src"),
        P(None, "tile", None),
        P(None, "tile", None),
        P("tile", "src"),
        P(None, "tile", "src"),
        P(),
        P(),
    )
    out_specs = (P(None, "tile", "src"), P("tile"))
    return jax.shard_map(shards, mesh=mesh, in_specs=in_specs, out_specs=out_specs, check_vma=False)
```

time: 1490 us -> 101 us (0.07)
  waiting for transfers between devices: 1070 us -> 0 us
  blocking collectives: 338 us -> 0 us
  Pallas kernels: 0 us -> 92.2 us
  local copies, waits for them, and re-layouts: 27.5 us -> 7.42 us
    unnamed x12 -> x0, waiting for transfers between devices: 582 us -> none
    reduce_scatter x3 -> x0, waiting for transfers between devices: 439 us -> none  [shards(): lax.psum_scatter(coupling(jnp.int32(0), part_rows * lax.axis_size('tile')...]
    all_gather x7 -> x0, blocking collectives: 292 us -> none  [the longest x4 172 us: shards(): lax.all_gather(residual, 'tile', axis=0, tiled=True)]
    pallas_call x0 -> x1, Pallas kernels: none -> 92.2 us  [shards(): pl.pallas_call(kernel, out_shape=(jax.ShapeDtypeStruct((PANELS, PART, 256...]
    all_gather x1 -> x0, waiting for transfers between devices: 54.1 us -> none  [shards(): lax.all_gather(wavefield, 'tile', axis=1, tiled=True).reshape(-1, sources)]
    psum x1 -> x0, blocking collectives: 46.2 us -> none  [shards(): total = lax.psum(partial_sum, 'src')]
    gather x1 -> x0, local copies, waits for them, and re-layouts: 17 us -> none  [shards(): ordered = jnp.take(gathered, cell_row, axis=0)]
  transfers between devices with their start and end apart: 10 -> 0, of which waited for: 8 -> 0; matrix products, arithmetic and copies ran while one was open for 0% -> 0% of each run, Pallas kernels for 0% -> 0%
where the time goes in v1:
time: 101 us; the launch traced here: 100 us
  Pallas kernels  92.2 us (91%)
  local copies, waits for them, and re-layouts  7.42 us (7%)
    pallas_call x1, Pallas kernels, shards(): pl.pallas_call(kernel, out_shape=(jax.ShapeDtypeStruct((PANELS, PART, 256...  92.2 us
    unnamed x16, local copies, waits for them, and re-layouts  7.42 us

profile of v1, /device:TPU:1, one launch (start us, length us, event | category | flops | bytes accessed | tf_op | source)
XLA Modules:
  0.0 100.3 jit_solution(538713696905411383)
XLA Ops:
  0.6 0.0 copy-start
  0.6 1.0 %copy-done = f32[27,4096]{1,0:T(8,128)S(1)} copy-done((f32[27,4096]{1,0:T(8,128)S(1)}, f32[27,4096]{1,0:T(8,128)}, u32[]{:S(2)}) %copy-start) | copy-done | bytes 442392
  1.7 0.0 copy-start.1
  1.7 1.0 copy-done.1
  2.7 0.0 copy-start.2
  2.7 0.9 copy-done.2
  3.6 0.0 copy-start.3
  3.6 0.9 copy-done.3
  4.5 0.0 copy-start.4
  4.5 0.8 copy-done.4
  5.4 0.0 copy-start.5
  5.4 0.8 copy-done.5
  6.2 0.0 copy-start.6
  6.2 0.7 copy-done.6
  6.9 92.2 %shard_map.86 = (bf16[4,32,256]{2,1,0:T(8,128)(2,1)S(1)}, f32[1,128]{1,0:T(1,128)S(1)}) custom-call(bf16[4,32,256]{2,1,0:T(8,128)(2,1)S(1)} %copy-done.4, bf16[6,32,1024]{2,1,0:T(8,128)(2,1)S(1)} %copy-done.1, bf16[4,32,1024]{2,1,0:T(8,128)(2,1)S(1)} %copy-done.2, bf16[128,256]{1,0:T(8,128)(2,1)S(1)} %copy-done.5, bf16[2,128,256]{2,1,0:T(8,128)(2,1)S(1)} %copy-done.3, ...), custom_call_target="tpu_custom_call" | custom-call | flops 1000000000 | bytes 4000000 | tf_op jit(solution)/shard_map/pallas_call | solution.py:354
  99.2 0.6 copy.11
  99.8 0.5 copy.12
Async XLA Ops:
  0.6 1.0 %copy-start = (f32[27,4096]{1,0:T(8,128)S(1)}, f32[27,4096]{1,0:T(8,128)}, u32[]{:S(2)}) copy-start(f32[27,4096]{1,0:T(8,128)} %coef.1) | copy-start | bytes 1327108
  1.7 1.0 copy-start.1
  2.7 0.9 copy-start.2
  3.6 0.9 copy-start.3
  4.5 0.8 copy-start.4
  5.4 0.8 copy-start.5
  6.2 0.7 copy-start.6

commit v2 on v1

v2 whole, which is shorter than its diff:
```python
import functools

import jax
import jax.numpy as jnp
from jax import lax
from jax.experimental import pallas as pl
from jax.experimental.pallas import tpu as pltpu
from jax.sharding import PartitionSpec as P

MESH = pl.DeviceIdType.MESH
F32 = jnp.float32
BF16 = jnp.bfloat16
NY = 4
NC = 8
PANELS = 4
PART = 32
SRC = 32
QUARTER = 256
PW = 1024
WIDE = 1280
NN = (((1,), (0,)), ((), ()))
NT = (((1,), (1,)), ((), ()))

ORDER = [("d", 0), ("l", 0), ("d", 1), ("l", 1), ("l", 2), ("d", 2), ("l", 3), ("l", 4), ("l", 5), ("d", 3)]
QUARTERED = [(), (), (2,), (0, 1, 2), (2,), (0, 1, 2), (2,), (0, 1, 2), (2,), (0, 1, 2)]
PLACE = {unit: number for number, unit in enumerate(ORDER)}


def block_of(later, earlier):
    return later * (later - 1) // 2 + earlier


def dot(a, b, dims):
    return lax.dot_general(a, b, dims, preferred_element_type=F32)


def kernel(
    rhs, lower, dinv, adj, side, coef_all, cells_all,
    wave_out, grad_out,
    rhs_in, adj_in, side_in, coef, cells,
    dcols, lrows, x_send, x_got, s_send, s_got, halo, order, perm, acc,
    part_send, part_got, y_full, z_own, z_all, grid, field, w_send, w_got,
    g1_send, g1_got, g2_send, g2_got,
    in_s, dy_s, dy_r, xa_s, xa_r, sa_s, sa_r, mo_s, mz_r, mq_r, mx_r, mc_r, st_s, st_r,
    za_s, za_r, ha_s, ha_r, wf_s, wf_r, g1_s, g1_r, g2_s, g2_r, tick,
):
    s = lax.axis_index("src")
    t = lax.axis_index("tile")
    x, zh = lax.rem(s, 4), lax.div(s, 4)
    y, zc = lax.div(t, NC), lax.rem(t, NC)
    zl, core = lax.div(zc, 2), lax.rem(zc, 2)
    z = zh * 4 + zl

    def dev(x, y, z, c):
        return (lax.div(z, 4) * 4 + x, (y * 4 + lax.rem(z, 4)) * 2 + c)

    def y_peer(d):
        return dev(x, lax.rem(y + d, NY), z, core)

    def x_peer(d):
        return dev(lax.rem(x + d, 4), y, z, core)

    def z_peer(d):
        return dev(x, y, lax.rem(z + d + 16, 16), core)

    def c_index(d):
        return lax.rem(zc + d, NC)

    def c_peer(d):
        return (s, y * NC + c_index(d))

    def s_peer(d):
        return (lax.rem(s + d, 16), t)

    sibling = dev(x, y, z, 1 - core)

    def send(src, dst, send_sem, recv_sem, device):
        pltpu.make_async_remote_copy(
            src_ref=src, dst_ref=dst, send_sem=send_sem, recv_sem=recv_sem,
            device_id=device, device_id_type=MESH,
        ).start()

    def received(ref, sem):
        pltpu.make_async_remote_copy(
            src_ref=ref, dst_ref=ref, send_sem=sem, recv_sem=sem,
            device_id=sibling, device_id_type=MESH,
        ).wait_recv()

    def sent(ref, sem):
        pltpu.make_async_remote_copy(
            src_ref=ref, dst_ref=ref, send_sem=sem, recv_sem=sem,
            device_id=sibling, device_id_type=MESH,
        ).wait_send()

    def signal(sem, device):
        pl.semaphore_signal(sem, inc=1, device_id=device, device_id_type=MESH)

    barrier = pltpu.get_barrier_semaphore()
    peers = [y_peer(d) for d in (1, 2, 3)] + [c_peer(d) for d in range(1, NC)]
    peers += [z_peer(d) for d in (1, -1, 2, -2)] + [x_peer(d) for d in (1, 2, 3)]
    for peer in peers:
        signal(barrier, peer)

    own_cols = pl.ds(pl.multiple_of(y * QUARTER, QUARTER), QUARTER)
    own_rows = pl.ds(pl.multiple_of(zc * SRC, SRC), SRC)
    own_cells = pl.ds(pl.multiple_of(y * PW, PW), PW)
    loads = [
        pltpu.make_async_copy(rhs, rhs_in, in_s.at[0]),
        pltpu.make_async_copy(dinv.at[:, :, own_cols], dcols.at[:, y, zc], in_s.at[1]),
        pltpu.make_async_copy(lower, lrows.at[:, zc], in_s.at[2]),
        pltpu.make_async_copy(cells_all, cells, in_s.at[3]),
        pltpu.make_async_copy(adj, adj_in, in_s.at[4]),
        pltpu.make_async_copy(side, side_in, in_s.at[5]),
        pltpu.make_async_copy(coef_all.at[:, own_cells], coef, in_s.at[6]),
    ]
    for load in loads:
        load.start()
    loads[0].wait()
    x_send[...] = rhs_in[...].astype(F32).reshape(PANELS * PART, 256).T.astype(BF16)
    x_got[zc] = x_send[own_rows, :]
    loads[1].wait()
    loads[2].wait()
    pl.semaphore_wait(barrier, len(peers))

    def spread(j):
        for d in (1, 2, 3):
            cols = pl.ds(pl.multiple_of(lax.rem(y + d, NY) * QUARTER, QUARTER), QUARTER)
            send(dinv.at[j, :, cols], dcols.at[j, y, zc], dy_s.at[j], dy_r.at[j], y_peer(d))

    spread(0)
    for d in range(1, NC):
        part = pl.ds(pl.multiple_of(c_index(d) * SRC, SRC), SRC)
        send(x_send.at[part, :], x_got.at[zc], xa_s, xa_r, c_peer(d))

    def unit_ref(unit, slot):
        kind, number = unit
        return dcols.at[number, :, slot] if kind == "d" else lrows.at[number, slot]

    def unit_slots(unit, count):
        kind, number = unit
        return dcols.at[number, :, pl.ds(0, count)] if kind == "d" else lrows.at[number, pl.ds(0, count)]

    def quarter_ref(unit, slot):
        kind, number = unit
        if kind == "d":
            return dcols.at[number, x, slot]
        return lrows.at[number, slot, :, pl.ds(pl.multiple_of(x * QUARTER, QUARTER), QUARTER)]

    def quarters(count):
        rows, columns = {1: (1, 1), 2: (1, 2), 3: (3, 1), 6: (3, 2), 9: (3, 3)}[count]
        return dcols.at[0, pl.ds(0, rows), pl.ds(0, columns)]

    def slot_at(d):
        return lax.rem(zl + d, 4) * 2 + core

    from_slots = (3, 1, 2)

    def push(unit):
        n = PLACE[unit]
        if unit[0] == "d":
            received(dcols.at[unit[1], pl.ds(0, 3), 0], dy_r.at[unit[1]])
        far = 2 - 4 * lax.rem(core + n, 2)
        for k, d in enumerate((1, -1, far)):
            if k in QUARTERED[n]:
                ref, sem = quarter_ref(unit, zc), mq_r
            else:
                ref, sem = unit_ref(unit, zc), mz_r
            send(ref, ref, mo_s.at[n], sem.at[n], z_peer(d))
        mine = unit_ref(unit, zc)
        send(mine, mine, mo_s.at[n], mc_r.at[n], sibling)

    def to_sibling(unit, k):
        here = unit_ref(unit, slot_at(from_slots[k]))
        send(here, here, mo_s.at[PLACE[unit]], mc_r.at[PLACE[unit]], sibling)

    def pump(unit):
        n = PLACE[unit]
        if QUARTERED[n]:
            received(quarters(len(QUARTERED[n])), mq_r.at[n])
            for k in QUARTERED[n]:
                here = quarter_ref(unit, slot_at(from_slots[k]))
                for d in (1, 2, 3):
                    send(here, here, mo_s.at[n], mx_r.at[n], x_peer(d))
        direct = [k for k in range(3) if k not in QUARTERED[n]]
        if direct:
            received(unit_slots(unit, len(direct)), mz_r.at[n])
            for k in direct:
                to_sibling(unit, k)

    def finish(unit):
        n = PLACE[unit]
        received(quarters(3 * len(QUARTERED[n])), mx_r.at[n])
        for k in QUARTERED[n]:
            to_sibling(unit, k)

    def ready(unit):
        received(unit_slots(unit, 4), mc_r.at[PLACE[unit]])

    push(("l", 0))
    for j in (1, 2, 3):
        spread(j)
    for unit in ORDER:
        if unit != ("l", 0):
            push(unit)

    for d in (2, -2):
        signal(tick.at[0], z_peer(d))

    loads[4].wait()
    loads[5].wait()
    s_send[:, 0:128] = adj_in[...].astype(F32).T.astype(BF16)
    s_send[:, 128:256] = side_in[0].astype(F32).T.astype(BF16)
    s_send[:, 256:384] = side_in[1].astype(F32).T.astype(BF16)
    s_got[zc] = s_send[own_rows, :]
    for d in range(1, NC):
        part = pl.ds(pl.multiple_of(c_index(d) * SRC, SRC), SRC)
        send(s_send.at[part, :], s_got.at[zc], sa_s, sa_r, c_peer(d))

    loads[3].wait()
    order[0:8, :] = cells[pl.ds(pl.multiple_of(lax.rem(y + 3, NY) * 8, 8), 8), :]
    left = jnp.where(y == 0, -1, order[7:8, :])
    order[8:16, :] = cells[pl.ds(pl.multiple_of(lax.rem(y + 1, NY) * 8, 8), 8), :]
    right = jnp.where(y == NY - 1, -1, order[8:9, :])
    middle = cells[pl.ds(pl.multiple_of(y * 8, 8), 8), :]
    wanted = [left] + [middle[i:i + 1, :] for i in range(8)] + [right]

    def fill(i, carry):
        rows = lax.broadcasted_iota(jnp.int32, (QUARTER, 128), 0) + i * QUARTER
        at = pl.ds(pl.multiple_of(i * QUARTER, QUARTER), QUARTER)
        for n, row in enumerate(wanted):
            hit = jnp.where(rows == row, 1.0, 0.0).astype(BF16)
            perm[at, n * 128:(n + 1) * 128] = hit
        return carry

    lax.fori_loop(0, 16, fill, 0)

    lane = lax.broadcasted_iota(jnp.int32, (SRC, 128), 1)
    received(x_got.at[pl.ds(0, NC - 1)], xa_r)
    for p in range(PANELS):
        for half in range(2):
            block = jnp.zeros((SRC, 128), F32)
            for q in range(4):
                piece = pltpu.roll(x_got[half * 4 + q].astype(F32), ((q - p) * PART) % 128, 1)
                block = jnp.where(lane // PART == q, piece, block)
            acc[p, :, half * 128:(half + 1) * 128] = block

    def share(step, value):
        part_send[step] = value.astype(BF16)
        for d in (1, 2, 3):
            send(part_send.at[step], part_got.at[step, d - 1], st_s.at[step], st_r.at[step], y_peer(d))

    def total(step):
        received(part_got.at[step], st_r.at[step])
        value = part_send[step].astype(F32)
        for d in range(3):
            value = value + part_got[step, d].astype(F32)
        return value

    def d_whole(j):
        return dcols[j].reshape(PW, QUARTER)

    def l_whole(later, earlier):
        return lrows[block_of(later, earlier)].reshape(QUARTER, PW)

    def take(later, earlier):
        acc[later] = acc[later] - dot(y_full[earlier], l_whole(later, earlier), NT)

    pump(("d", 0))
    pump(("l", 0))
    ready(("d", 0))
    for j in range(PANELS):
        share(j, dot(acc[j].astype(BF16), d_whole(j), NT))
        if j == 0:
            pump(("d", 1))
            pump(("l", 1))
            finish(("d", 1))
            pump(("l", 2))
            ready(("l", 0))
            ready(("d", 1))
            pl.semaphore_wait(tick.at[0], 2)
            for d in (4, -4):
                signal(tick.at[1], z_peer(d))
        if j == 1:
            finish(("l", 1))
            finish(("l", 2))
            pump(("d", 2))
            pump(("l", 3))
            ready(("l", 1))
            take(2, 0)
            finish(("d", 2))
            pump(("l", 4))
            ready(("l", 2))
            ready(("d", 2))
            pl.semaphore_wait(tick.at[1], 2)
            for d in (1, 2, 3):
                signal(tick.at[2], x_peer(d))
        if j == 2:
            finish(("l", 3))
            pump(("l", 5))
            finish(("l", 4))
            pump(("d", 3))
            ready(("l", 3))
            take(3, 0)
            ready(("l", 4))
            take(3, 1)
            finish(("l", 5))
            finish(("d", 3))
            ready(("l", 5))
            ready(("d", 3))
        if j == 3:
            pl.semaphore_wait(tick.at[2], 3)
            received(s_got.at[pl.ds(0, NC - 1)], sa_r)
            send(s_got.at[7, :, pl.ds(128, 256)], halo.at[0], ha_s, ha_r, y_peer(1))
            send(s_got.at[0, :, pl.ds(128, 256)], halo.at[1], ha_s, ha_r, y_peer(3))
        y_full[j] = total(j).astype(BF16)
        if j + 1 < PANELS:
            take(j + 1, j)

    loads[6].wait()
    zpos = lax.rem(lax.broadcasted_iota(jnp.int32, (1, PW), 1), 64)

    def stencil(plane, offset_x):
        value = jnp.zeros((SRC, PW), F32)
        for offset_y in (-1, 0, 1):
            for offset_z in (-1, 0, 1):
                number = (offset_x + 1) * 9 + (offset_y + 1) * 3 + (offset_z + 1)
                weight = coef[number:number + 1, :]
                if offset_z == -1:
                    weight = jnp.where(zpos > 0, weight, 0.0)
                if offset_z == 1:
                    weight = jnp.where(zpos < 63, weight, 0.0)
                shift = offset_y * 64 + offset_z
                near = pltpu.roll(plane, (-shift) % WIDE, 1) if shift else plane
                value = value + weight * near[:, 128:128 + PW]
        return value

    def side_plane(n):
        low = 128 * (n + 1)
        first = jnp.where(y == 0, 0.0, halo[0, :, 128 * n:128 * (n + 1)].astype(F32))
        last = jnp.where(y == NY - 1, 0.0, halo[1, :, 128 * n:128 * (n + 1)].astype(F32))
        inner = [s_got[i, :, low:low + 128].astype(F32) for i in range(NC)]
        return jnp.concatenate([first] + inner + [last], axis=1)

    def order_cells(j):
        received(z_all.at[j, pl.ds(0, 3)], za_r.at[j])
        value = jnp.zeros((SRC, WIDE), F32)
        for q in range(NY):
            rows = slice((j * NY + q) * QUARTER, (j * NY + q + 1) * QUARTER)
            value = value + dot(z_all[j, q], perm[rows, :], NN)
        return value

    later_term = {}
    whole = y_full[3]
    for j in reversed(range(PANELS)):
        z_j = dot(whole, d_whole(j), NN).astype(BF16)
        z_own[j] = z_j
        if j > 0:
            term = dot(z_j, l_whole(j, j - 1), NN)
            if j - 1 in later_term:
                term = term + later_term[j - 1]
            share(7 - j, term)
        z_all[j, y] = z_j
        for d in (1, 2, 3):
            send(z_own.at[j], z_all.at[j, y], za_s.at[j], za_r.at[j], y_peer(d))
        if j > 0:
            for earlier in range(j - 1):
                more = dot(z_j, l_whole(j, earlier), NN)
                later_term[earlier] = later_term[earlier] + more if earlier in later_term else more
            if j == 3:
                received(halo, ha_r)
                field[...] = stencil(side_plane(0), -1) + stencil(side_plane(1), 1)
            else:
                grid[...] = order_cells(j + 1) if j == 2 else grid[...] + order_cells(j + 1)
            whole = (y_full[j - 1].astype(F32) - total(7 - j)).astype(BF16)

    z_f32 = [z_own[p].astype(F32) for p in range(PANELS)]
    for n in range(NC):
        block = jnp.zeros((SRC, 128), F32)
        for p in range(PANELS):
            piece = z_f32[p][:, (n // 4) * 128:(n // 4 + 1) * 128]
            piece = pltpu.roll(piece, ((p - n % 4) * PART) % 128, 1)
            block = jnp.where(lane // PART == p, piece, block)
        w_send[n] = block.astype(BF16)
    w_got[zc] = w_send[zc]
    for d in range(1, NC):
        send(w_send.at[c_index(d)], w_got.at[zc], wf_s, wf_r, c_peer(d))

    grid[...] = grid[...] + order_cells(1)
    field_all = field[...] + stencil(grid[...] + order_cells(0), 0)
    for n in range(NC):
        here = s_got[n, :, 0:128].astype(F32) * field_all[:, n * 128:(n + 1) * 128]
        g1_send[n] = jnp.sum(here, axis=0, keepdims=True)

    for d in range(1, NC):
        send(g1_send.at[c_index(d)], g1_got.at[d - 1], g1_s, g1_r, c_peer(d))
    received(g1_got, g1_r)
    group = g1_send[zc]
    for d in range(1, NC):
        group = group + g1_got[d - 1]
    g2_send[...] = group
    for d in range(1, 16):
        send(g2_send, g2_got.at[d - 1], g2_s, g2_r, s_peer(d))

    received(w_got.at[pl.ds(0, NC - 1)], wf_r)
    back = w_got[...].astype(F32).reshape(256, 128).T
    wave_out[...] = back.reshape(PANELS, PART, 256).astype(BF16)

    for j in range(PANELS):
        sent(dcols.at[j, pl.ds(0, 3), 0], dy_s.at[j])
        sent(z_all.at[j, pl.ds(0, 3)], za_s.at[j])
    sent(x_got.at[pl.ds(0, NC - 1)], xa_s)
    sent(s_got.at[pl.ds(0, NC - 1)], sa_s)
    for n in range(len(ORDER)):
        sent(lrows.at[0, pl.ds(0, 7)], mo_s.at[n])
    for step in range(7):
        sent(part_got.at[step], st_s.at[step])
    sent(halo, ha_s)
    sent(w_got.at[pl.ds(0, NC - 1)], wf_s)
    sent(g1_got, g1_s)

    received(g2_got, g2_r)
    for d in range(1, 16):
        group = group + g2_got[d - 1]
    grad_out[...] = group * (1.0 / 64.0)
    sent(g2_got, g2_s)


def shards(rhs, lower_blocks, dinv, adjoint_field, side_field, stencil_coef, cell_row):
    dma = pltpu.SemaphoreType.DMA
    units = (len(ORDER),)
    wavefield, gradient = pl.pallas_call(
        kernel,
        out_shape=(
            jax.ShapeDtypeStruct((PANELS, PART, 256), BF16),
            jax.ShapeDtypeStruct((1, 128), F32),
        ),
        in_specs=[pl.BlockSpec(memory_space=pl.ANY)] * 7,
        out_specs=(pl.BlockSpec(memory_space=pltpu.VMEM),) * 2,
        scratch_shapes=[
            pltpu.VMEM((PANELS, PART, 256), BF16),
            pltpu.VMEM((128, 256), BF16),
            pltpu.VMEM((2, 128, 256), BF16),
            pltpu.VMEM((27, PW), F32),
            pltpu.VMEM((32, 128), jnp.int32),
            pltpu.VMEM((PANELS, NY, NC, PART, QUARTER), BF16),
            pltpu.VMEM((6, NC, PART, PW), BF16),
            pltpu.VMEM((256, 128), BF16),
            pltpu.VMEM((NC, SRC, 128), BF16),
            pltpu.VMEM((256, 384), BF16),
            pltpu.VMEM((NC, SRC, 384), BF16),
            pltpu.VMEM((2, SRC, 256), BF16),
            pltpu.VMEM((16, 128), jnp.int32),
            pltpu.VMEM((4096, WIDE), BF16),
            pltpu.VMEM((PANELS, SRC, QUARTER), F32),
            pltpu.VMEM((7, SRC, PW), BF16),
            pltpu.VMEM((7, 3, SRC, PW), BF16),
            pltpu.VMEM((PANELS, SRC, PW), BF16),
            pltpu.VMEM((PANELS, SRC, QUARTER), BF16),
            pltpu.VMEM((PANELS, NY, SRC, QUARTER), BF16),
            pltpu.VMEM((SRC, WIDE), F32),
            pltpu.VMEM((SRC, PW), F32),
            pltpu.VMEM((NC, SRC, 128), BF16),
            pltpu.VMEM((NC, SRC, 128), BF16),
            pltpu.VMEM((NC, 1, 128), F32),
            pltpu.VMEM((NC - 1, 1, 128), F32),
            pltpu.VMEM((1, 128), F32),
            pltpu.VMEM((15, 1, 128), F32),
            dma((7,)),
            dma((PANELS,)), dma((PANELS,)),
            dma, dma,
            dma, dma,
            dma(units), dma(units), dma(units), dma(units), dma(units),
            dma((7,)), dma((7,)),
            dma((PANELS,)), dma((PANELS,)),
            dma, dma,
            dma, dma,
            dma, dma,
            dma, dma,
            pltpu.SemaphoreType.REGULAR((3,)),
        ],
        compiler_params=pltpu.CompilerParams(
            collective_id=0, has_side_effects=True, vmem_limit_bytes=64 * 1024 * 1024
        ),
        cost_estimate=pl.CostEstimate(flops=10**9, bytes_accessed=4 * 10**6, transcendentals=0),
    )(rhs, lower_blocks, dinv, adjoint_field, side_field, stencil_coef, cell_row.reshape(32, 128))
    return wavefield, gradient.reshape(128)


def solution(mesh):
    in_specs = (
        P(None, "tile", "src"),
        P(None, "tile", None),
        P(None, "tile", None),
        P("tile", "src"),
        P(None, "tile", "src"),
        P(),
        P(),
    )
    out_specs = (P(None, "tile", "src"), P("tile"))
    return jax.shard_map(shards, mesh=mesh, in_specs=in_specs, out_specs=out_specs, check_vma=False)
```

time: 101 us -> 92.5 us (0.916)
  local copies, waits for them, and re-layouts: 7.42 us -> 1.99 us
  Pallas kernels: 92.2 us -> 89.7 us
    unnamed x16 -> x4, local copies, waits for them, and re-layouts: 7.42 us -> 1.99 us
    pallas_call x1, Pallas kernels: 92.2 us -> 89.7 us  [shards(): pl.pallas_call(kernel, out_shape=(jax.ShapeDtypeStruct((PANELS, PART, 256...]
where the time goes in v2:
time: 92.5 us; the launch traced here: 92.3 us
  Pallas kernels  89.7 us (97%)
  local copies, waits for them, and re-layouts  1.99 us (2%)
    pallas_call x1, Pallas kernels, shards(): pl.pallas_call(kernel, out_shape=(jax.ShapeDtypeStruct((PANELS, PART, 256...  89.7 us
    unnamed x4, local copies, waits for them, and re-layouts  1.99 us

profile of v2, /device:TPU:1, one launch (start us, length us, event | category | flops | bytes accessed | tf_op | source)
XLA Modules:
  0.0 92.3 jit_solution(6945257108719165781)
XLA Ops:
  0.6 89.7 %shard_map.86 = (bf16[4,32,256]{2,1,0:T(8,128)(2,1)}, f32[1,128]{1,0:T(1,128)}) custom-call(bf16[4,32,256]{2,1,0:T(8,128)(2,1)} %rhs.1, bf16[6,32,1024]{2,1,0:T(8,128)(2,1)} %lower.1, bf16[4,32,1024]{2,1,0:T(8,128)(2,1)} %dinv.1, bf16[128,256]{1,0:T(8,128)(2,1)} %adj.1, bf16[2,128,256]{2,1,0:T(8,128)(2,1)} %side.1, f32[27,4096]{1,0:T(8,128)} %coef_all.1, ...), custom_call_target="tpu_custom_call" | custom-call | flops 1000000000 | bytes 4000000 | tf_op jit(solution)/shard_map/pallas_call | solution.py:431
  90.3 0.0 copy-start
  90.3 1.5 %copy.11 = bf16[4,32,256]{2,1,0:T(8,128)(2,1)} copy(bf16[4,32,256]{2,1,0:T(8,128)(2,1)} %get-tuple-element.8) | data formatting | bytes 131072
  91.8 0.0 copy-done
  91.8 0.5 copy.12
Async XLA Ops:
  90.3 1.5 %copy-start = (f32[1,128]{1,0:T(1,128)S(1)}, f32[1,128]{1,0:T(1,128)}, u32[]{:S(2)}) copy-start(f32[1,128]{1,0:T(1,128)} %get-tuple-element.5) | copy-start | bytes 1540

commit v3 on v2

--- a/solution.py
+++ b/solution.py
@@ -14,6 +14,7 @@
 NC = 8
 PANELS = 4
 PART = 32
+HALF = 16
 SRC = 32
 QUARTER = 256
 PW = 1024
@@ -22,7 +23,26 @@
 NT = (((1,), (1,)), ((), ()))
 
 ORDER = [("d", 0), ("l", 0), ("d", 1), ("l", 1), ("l", 2), ("d", 2), ("l", 3), ("l", 4), ("l", 5), ("d", 3)]
-QUARTERED = [(), (), (2,), (0, 1, 2), (2,), (0, 1, 2), (2,), (0, 1, 2), (2,), (0, 1, 2)]
+QUARTERED = [(), (), (), (2,), (2,), (2,), (2,), (2,), (2,), (2,)]
+SCHEDULE = {
+    "start": [
+        "push l0", "push d0", "spread d1", "spread d2", "spread d3", "push d1", "push l1",
+    ],
+    "first": [
+        "pump d0", "push l2", "pump l0", "ready d0",
+    ],
+    0: [
+        "pump d1", "push d2", "pump l1", "push l3", "finish d1", "push l4", "ready l0", "ready d1",
+    ],
+    1: [
+        "pump l2", "push l5", "finish l1", "pump d2", "push d3", "finish l2", "pump l3", "ready l1",
+        "take l20", "finish d2", "pump l4", "ready l2", "ready d2",
+    ],
+    2: [
+        "finish l3", "pump l5", "finish l4", "pump d3", "ready l3", "take l30", "ready l4", "take l31",
+        "finish l5", "finish d3", "ready l5", "ready d3",
+    ],
+}
 PLACE = {unit: number for number, unit in enumerate(ORDER)}
 
 
@@ -189,6 +209,8 @@
 
     def finish(unit):
         n = PLACE[unit]
+        if not QUARTERED[n]:
+            return
         received(quarters(3 * len(QUARTERED[n])), mx_r.at[n])
         for k in QUARTERED[n]:
             to_sibling(unit, k)
@@ -196,12 +218,27 @@
     def ready(unit):
         received(unit_slots(unit, 4), mc_r.at[PLACE[unit]])
 
-    push(("l", 0))
-    for j in (1, 2, 3):
-        spread(j)
-    for unit in ORDER:
-        if unit != ("l", 0):
-            push(unit)
+    def run(name):
+        for step in SCHEDULE.get(name, ""):
+            verb, what = step.split()
+            kind, number = what[0], int(what[1:])
+            if verb == "spread":
+                spread(number)
+            elif verb == "take":
+                take(number // 10, number % 10)
+            else:
+                {"push": push, "pump": pump, "finish": finish, "ready": ready}[verb]((kind, number))
+
+    def d_whole(j):
+        return dcols[j].reshape(PW, QUARTER)
+
+    def l_whole(later, earlier):
+        return lrows[block_of(later, earlier)].reshape(QUARTER, PW)
+
+    def take(later, earlier):
+        acc[later] = acc[later] - dot(y_full[earlier], l_whole(later, earlier), NT)
+
+    run("start")
 
     for d in (2, -2):
         signal(tick.at[0], z_peer(d))
@@ -212,9 +249,6 @@
     s_send[:, 128:256] = side_in[0].astype(F32).T.astype(BF16)
     s_send[:, 256:384] = side_in[1].astype(F32).T.astype(BF16)
     s_got[zc] = s_send[own_rows, :]
-    for d in range(1, NC):
-        part = pl.ds(pl.multiple_of(c_index(d) * SRC, SRC), SRC)
-        send(s_send.at[part, :], s_got.at[zc], sa_s, sa_r, c_peer(d))
 
     loads[3].wait()
     order[0:8, :] = cells[pl.ds(pl.multiple_of(lax.rem(y + 3, NY) * 8, 8), 8), :]
@@ -244,77 +278,45 @@
                 block = jnp.where(lane // PART == q, piece, block)
             acc[p, :, half * 128:(half + 1) * 128] = block
 
-    def share(step, value):
-        part_send[step] = value.astype(BF16)
+    def share(step, half, value):
+        part_send[step, half] = value.astype(BF16)
+        n = step * 2 + half
         for d in (1, 2, 3):
-            send(part_send.at[step], part_got.at[step, d - 1], st_s.at[step], st_r.at[step], y_peer(d))
-
-    def total(step):
-        received(part_got.at[step], st_r.at[step])
-        value = part_send[step].astype(F32)
+            send(part_send.at[step, half], part_got.at[step, half, d - 1], st_s.at[n], st_r.at[n], y_peer(d))
+
+    def total(step, half):
+        received(part_got.at[step, half], st_r.at[step * 2 + half])
+        value = part_send[step, half].astype(F32)
         for d in range(3):
-            value = value + part_got[step, d].astype(F32)
+            value = value + part_got[step, half, d].astype(F32)
         return value
 
-    def d_whole(j):
-        return dcols[j].reshape(PW, QUARTER)
-
-    def l_whole(later, earlier):
-        return lrows[block_of(later, earlier)].reshape(QUARTER, PW)
-
-    def take(later, earlier):
-        acc[later] = acc[later] - dot(y_full[earlier], l_whole(later, earlier), NT)
-
-    pump(("d", 0))
-    pump(("l", 0))
-    ready(("d", 0))
+    halves = [slice(0, HALF), slice(HALF, SRC)]
+
+    run("first")
     for j in range(PANELS):
-        share(j, dot(acc[j].astype(BF16), d_whole(j), NT))
+        for half, some in enumerate(halves):
+            if j > 0:
+                y_full[j - 1, some, :] = total(j - 1, half).astype(BF16)
+                acc[j, some, :] = acc[j, some, :] - dot(y_full[j - 1, some, :], l_whole(j, j - 1), NT)
+            share(j, half, dot(acc[j, some, :].astype(BF16), d_whole(j), NT))
+        run(j)
         if j == 0:
-            pump(("d", 1))
-            pump(("l", 1))
-            finish(("d", 1))
-            pump(("l", 2))
-            ready(("l", 0))
-            ready(("d", 1))
             pl.semaphore_wait(tick.at[0], 2)
             for d in (4, -4):
                 signal(tick.at[1], z_peer(d))
         if j == 1:
-            finish(("l", 1))
-            finish(("l", 2))
-            pump(("d", 2))
-            pump(("l", 3))
-            ready(("l", 1))
-            take(2, 0)
-            finish(("d", 2))
-            pump(("l", 4))
-            ready(("l", 2))
-            ready(("d", 2))
+            for d in range(1, NC):
+                part = pl.ds(pl.multiple_of(c_index(d) * SRC, SRC), SRC)
+                send(s_send.at[part, :], s_got.at[zc], sa_s, sa_r, c_peer(d))
             pl.semaphore_wait(tick.at[1], 2)
             for d in (1, 2, 3):
                 signal(tick.at[2], x_peer(d))
-        if j == 2:
-            finish(("l", 3))
-            pump(("l", 5))
-            finish(("l", 4))
-            pump(("d", 3))
-            ready(("l", 3))
-            take(3, 0)
-            ready(("l", 4))
-            take(3, 1)
-            finish(("l", 5))
-            finish(("d", 3))
-            ready(("l", 5))
-            ready(("d", 3))
         if j == 3:
             pl.semaphore_wait(tick.at[2], 3)
             received(s_got.at[pl.ds(0, NC - 1)], sa_r)
             send(s_got.at[7, :, pl.ds(128, 256)], halo.at[0], ha_s, ha_r, y_peer(1))
             send(s_got.at[0, :, pl.ds(128, 256)], halo.at[1], ha_s, ha_r, y_peer(3))
-        y_full[j] = total(j).astype(BF16)
-        if j + 1 < PANELS:
-            take(j + 1, j)
 
     loads[6].wait()
     zpos = lax.rem(lax.broadcasted_iota(jnp.int32, (1, PW), 1), 64)
@@ -350,15 +352,20 @@
         return value
 
     later_term = {}
-    whole = y_full[3]
     for j in reversed(range(PANELS)):
-        z_j = dot(whole, d_whole(j), NN).astype(BF16)
-        z_own[j] = z_j
-        if j > 0:
-            term = dot(z_j, l_whole(j, j - 1), NN)
-            if j - 1 in later_term:
-                term = term + later_term[j - 1]
-            share(7 - j, term)
+        for half, some in enumerate(halves):
+            if j == 3:
+                whole = total(3, half).astype(BF16)
+            else:
+                whole = (y_full[j, some, :].astype(F32) - total(6 - j, half)).astype(BF16)
+            z_some = dot(whole, d_whole(j), NN).astype(BF16)
+            z_own[j, some, :] = z_some
+            if j > 0:
+                term = dot(z_some, l_whole(j, j - 1), NN)
+                if j - 1 in later_term:
+                    term = term + later_term[j - 1][some]
+                share(7 - j, half, term)
+        z_j = z_own[j]
         z_all[j, y] = z_j
         for d in (1, 2, 3):
             send(z_own.at[j], z_all.at[j, y], za_s.at[j], za_r.at[j], y_peer(d))
@@ -371,7 +378,6 @@
                 field[...] = stencil(side_plane(0), -1) + stencil(side_plane(1), 1)
             else:
                 grid[...] = order_cells(j + 1) if j == 2 else grid[...] + order_cells(j + 1)
-            whole = (y_full[j - 1].astype(F32) - total(7 - j)).astype(BF16)
 
     z_f32 = [z_own[p].astype(F32) for p in range(PANELS)]
     for n in range(NC):
@@ -413,7 +419,8 @@
     for n in range(len(ORDER)):
         sent(lrows.at[0, pl.ds(0, 7)], mo_s.at[n])
     for step in range(7):
-        sent(part_got.at[step], st_s.at[step])
+        for half in range(2):
+            sent(part_got.at[step, half], st_s.at[step * 2 + half])
     sent(halo, ha_s)
     sent(w_got.at[pl.ds(0, NC - 1)], wf_s)
     sent(g1_got, g1_s)
@@ -452,8 +459,8 @@
             pltpu.VMEM((16, 128), jnp.int32),
             pltpu.VMEM((4096, WIDE), BF16),
             pltpu.VMEM((PANELS, SRC, QUARTER), F32),
-            pltpu.VMEM((7, SRC, PW), BF16),
-            pltpu.VMEM((7, 3, SRC, PW), BF16),
+            pltpu.VMEM((7, 2, HALF, PW), BF16),
+            pltpu.VMEM((7, 2, 3, HALF, PW), BF16),
             pltpu.VMEM((PANELS, SRC, PW), BF16),
             pltpu.VMEM((PANELS, SRC, QUARTER), BF16),
             pltpu.VMEM((PANELS, NY, SRC, QUARTER), BF16),
@@ -470,7 +477,7 @@
             dma, dma,
             dma, dma,
             dma(units), dma(units), dma(units), dma(units), dma(units),
-            dma((7,)), dma((7,)),
+            dma((14,)), dma((14,)),
             dma((PANELS,)), dma((PANELS,)),
             dma, dma,
             dma, dma,

time: 92.5 us -> 85.1 us (0.920)
  Pallas kernels: 89.7 us -> 82.3 us
    pallas_call x1, Pallas kernels: 89.7 us -> 82.3 us  [shards(): pl.pallas_call(kernel, out_shape=(jax.ShapeDtypeStruct((PANELS, PART, 256...]
where the time goes in v3:
time: 85.1 us; the launch traced here: 84.9 us
  Pallas kernels  82.3 us (97%)
  local copies, waits for them, and re-layouts  1.99 us (2%)
    pallas_call x1, Pallas kernels, shards(): pl.pallas_call(kernel, out_shape=(jax.ShapeDtypeStruct((PANELS, PART, 256...  82.3 us
    unnamed x4, local copies, waits for them, and re-layouts  1.99 us

profile of v3, /device:TPU:1, one launch (start us, length us, event | category | flops | bytes accessed | tf_op | source)
XLA Modules:
  0.0 84.9 jit_solution(6683697511347988784)
XLA Ops:
  0.6 82.3 %shard_map.86 = (bf16[4,32,256]{2,1,0:T(8,128)(2,1)}, f32[1,128]{1,0:T(1,128)}) custom-call(bf16[4,32,256]{2,1,0:T(8,128)(2,1)} %rhs.1, bf16[6,32,1024]{2,1,0:T(8,128)(2,1)} %lower.1, bf16[4,32,1024]{2,1,0:T(8,128)(2,1)} %dinv.1, bf16[128,256]{1,0:T(8,128)(2,1)} %adj.1, bf16[2,128,256]{2,1,0:T(8,128)(2,1)} %side.1, f32[27,4096]{1,0:T(8,128)} %coef_all.1, ...), custom_call_target="tpu_custom_call" | custom-call | flops 1000000000 | bytes 4000000 | tf_op jit(solution)/shard_map/pallas_call | solution.py:438
  82.9 0.0 copy-start
  82.9 1.5 %copy.11 = bf16[4,32,256]{2,1,0:T(8,128)(2,1)} copy(bf16[4,32,256]{2,1,0:T(8,128)(2,1)} %get-tuple-element.8) | data formatting | bytes 131072
  84.4 0.0 copy-done
  84.4 0.5 copy.12
Async XLA Ops:
  82.9 1.5 %copy-start = (f32[1,128]{1,0:T(1,128)S(1)}, f32[1,128]{1,0:T(1,128)}, u32[]{:S(2)}) copy-start(f32[1,128]{1,0:T(1,128)} %get-tuple-element.5) | copy-start | bytes 1540

commit v4 on v3

--- a/solution.py
+++ b/solution.py
@@ -58,7 +58,7 @@
     rhs, lower, dinv, adj, side, coef_all, cells_all,
     wave_out, grad_out,
     rhs_in, adj_in, side_in, coef, cells,
-    dcols, lrows, x_send, x_got, s_send, s_got, halo, order, perm, acc,
+    dcols, lrows, x_send, x_got, s_send, s_got, halo, perm, acc,
     part_send, part_got, y_full, z_own, z_all, grid, field, w_send, w_got,
     g1_send, g1_got, g2_send, g2_got,
     in_s, dy_s, dy_r, xa_s, xa_r, sa_s, sa_r, mo_s, mz_r, mq_r, mx_r, mc_r, st_s, st_r,
@@ -143,12 +143,12 @@
     pl.semaphore_wait(barrier, len(peers))
 
     def spread(j):
-        for d in (1, 2, 3):
+        for d in (2, 1, 3):
             cols = pl.ds(pl.multiple_of(lax.rem(y + d, NY) * QUARTER, QUARTER), QUARTER)
             send(dinv.at[j, :, cols], dcols.at[j, y, zc], dy_s.at[j], dy_r.at[j], y_peer(d))
 
     spread(0)
-    for d in range(1, NC):
+    for d in (4, 3, 5, 6, 2, 7, 1):
         part = pl.ds(pl.multiple_of(c_index(d) * SRC, SRC), SRC)
         send(x_send.at[part, :], x_got.at[zc], xa_s, xa_r, c_peer(d))
 
@@ -180,7 +180,7 @@
         if unit[0] == "d":
             received(dcols.at[unit[1], pl.ds(0, 3), 0], dy_r.at[unit[1]])
         far = 2 - 4 * lax.rem(core + n, 2)
-        for k, d in enumerate((1, -1, far)):
+        for k, d in ((2, far), (0, 1), (1, -1)):
             if k in QUARTERED[n]:
                 ref, sem = quarter_ref(unit, zc), mq_r
             else:
@@ -199,7 +199,7 @@
             received(quarters(len(QUARTERED[n])), mq_r.at[n])
             for k in QUARTERED[n]:
                 here = quarter_ref(unit, slot_at(from_slots[k]))
-                for d in (1, 2, 3):
+                for d in (2, 1, 3):
                     send(here, here, mo_s.at[n], mx_r.at[n], x_peer(d))
         direct = [k for k in range(3) if k not in QUARTERED[n]]
         if direct:
@@ -251,12 +251,12 @@
     s_got[zc] = s_send[own_rows, :]
 
     loads[3].wait()
-    order[0:8, :] = cells[pl.ds(pl.multiple_of(lax.rem(y + 3, NY) * 8, 8), 8), :]
-    left = jnp.where(y == 0, -1, order[7:8, :])
-    order[8:16, :] = cells[pl.ds(pl.multiple_of(lax.rem(y + 1, NY) * 8, 8), 8), :]
-    right = jnp.where(y == NY - 1, -1, order[8:9, :])
-    middle = cells[pl.ds(pl.multiple_of(y * 8, 8), 8), :]
-    wanted = [left] + [middle[i:i + 1, :] for i in range(8)] + [right]
+    def cells_from(number):
+        return cells[pl.ds(pl.multiple_of(number * 128, 128), 128)].reshape(1, 128)
+
+    left = jnp.where(y == 0, -1, cells_from(lax.rem(y + 3, NY) * 8 + 7))
+    right = jnp.where(y == NY - 1, -1, cells_from(lax.rem(y + 1, NY) * 8))
+    wanted = [left] + [cells_from(y * 8 + i) for i in range(8)] + [right]
 
     def fill(i, carry):
         rows = lax.broadcasted_iota(jnp.int32, (QUARTER, 128), 0) + i * QUARTER
@@ -281,7 +281,7 @@
     def share(step, half, value):
         part_send[step, half] = value.astype(BF16)
         n = step * 2 + half
-        for d in (1, 2, 3):
+        for d in (2, 1, 3):
             send(part_send.at[step, half], part_got.at[step, half, d - 1], st_s.at[n], st_r.at[n], y_peer(d))
 
     def total(step, half):
@@ -367,7 +367,7 @@
                 share(7 - j, half, term)
         z_j = z_own[j]
         z_all[j, y] = z_j
-        for d in (1, 2, 3):
+        for d in (2, 1, 3):
             send(z_own.at[j], z_all.at[j, y], za_s.at[j], za_r.at[j], y_peer(d))
         if j > 0:
             for earlier in range(j - 1):
@@ -397,16 +397,8 @@
         here = s_got[n, :, 0:128].astype(F32) * field_all[:, n * 128:(n + 1) * 128]
         g1_send[n] = jnp.sum(here, axis=0, keepdims=True)
 
-    for d in range(1, NC):
+    for d in (4, 3, 5, 6, 2, 7, 1):
         send(g1_send.at[c_index(d)], g1_got.at[d - 1], g1_s, g1_r, c_peer(d))
-    received(g1_got, g1_r)
-    group = g1_send[zc]
-    for d in range(1, NC):
-        group = group + g1_got[d - 1]
-    g2_send[...] = group
-    for d in range(1, 16):
-        send(g2_send, g2_got.at[d - 1], g2_s, g2_r, s_peer(d))
-
     received(w_got.at[pl.ds(0, NC - 1)], wf_r)
     back = w_got[...].astype(F32).reshape(256, 128).T
     wave_out[...] = back.reshape(PANELS, PART, 256).astype(BF16)
@@ -423,8 +415,15 @@
             sent(part_got.at[step, half], st_s.at[step * 2 + half])
     sent(halo, ha_s)
     sent(w_got.at[pl.ds(0, NC - 1)], wf_s)
+    received(g1_got, g1_r)
+    group = g1_send[zc]
+    for d in range(1, NC):
+        group = group + g1_got[d - 1]
+    g2_send[...] = group
+    for d in (8, 7, 9, 10, 6, 4, 12, 5, 11, 3, 13, 14, 2, 1, 15):
+        send(g2_send, g2_got.at[d - 1], g2_s, g2_r, s_peer(d))
+
     sent(g1_got, g1_s)
-
     received(g2_got, g2_r)
     for d in range(1, 16):
         group = group + g2_got[d - 1]
@@ -448,7 +447,7 @@
             pltpu.VMEM((128, 256), BF16),
             pltpu.VMEM((2, 128, 256), BF16),
             pltpu.VMEM((27, PW), F32),
-            pltpu.VMEM((32, 128), jnp.int32),
+            pltpu.VMEM((4096,), jnp.int32),
             pltpu.VMEM((PANELS, NY, NC, PART, QUARTER), BF16),
             pltpu.VMEM((6, NC, PART, PW), BF16),
             pltpu.VMEM((256, 128), BF16),
@@ -456,7 +455,6 @@
             pltpu.VMEM((256, 384), BF16),
             pltpu.VMEM((NC, SRC, 384), BF16),
             pltpu.VMEM((2, SRC, 256), BF16),
-            pltpu.VMEM((16, 128), jnp.int32),
             pltpu.VMEM((4096, WIDE), BF16),
             pltpu.VMEM((PANELS, SRC, QUARTER), F32),
             pltpu.VMEM((7, 2, HALF, PW), BF16),
@@ -489,7 +487,7 @@
             collective_id=0, has_side_effects=True, vmem_limit_bytes=64 * 1024 * 1024
         ),
         cost_estimate=pl.CostEstimate(flops=10**9, bytes_accessed=4 * 10**6, transcendentals=0),
-    )(rhs, lower_blocks, dinv, adjoint_field, side_field, stencil_coef, cell_row.reshape(32, 128))
+    )(rhs, lower_blocks, dinv, adjoint_field, side_field, stencil_coef, cell_row)
     return wavefield, gradient.reshape(128)
 
 

time: 85.1 us -> 82.8 us (0.973)
  Pallas kernels: 82.3 us -> 80 us
    pallas_call x1, Pallas kernels: 82.3 us -> 80 us  [shards(): pl.pallas_call(kernel, out_shape=(jax.ShapeDtypeStruct((PANELS, PART, 256...]
where the time goes in v4:
time: 82.8 us; the launch traced here: 82.6 us
  Pallas kernels  80 us (97%)
  local copies, waits for them, and re-layouts  1.99 us (2%)
    pallas_call x1, Pallas kernels, shards(): pl.pallas_call(kernel, out_shape=(jax.ShapeDtypeStruct((PANELS, PART, 256...  80 us
    unnamed x4, local copies, waits for them, and re-layouts  1.99 us

profile of v4, /device:TPU:1, one launch (start us, length us, event | category | flops | bytes accessed | tf_op | source)
XLA Modules:
  0.0 82.6 jit_solution(8714447215541860324)
XLA Ops:
  0.6 80.0 %shard_map.86 = (bf16[4,32,256]{2,1,0:T(8,128)(2,1)}, f32[1,128]{1,0:T(1,128)}) custom-call(bf16[4,32,256]{2,1,0:T(8,128)(2,1)} %rhs.1, bf16[6,32,1024]{2,1,0:T(8,128)(2,1)} %lower.1, bf16[4,32,1024]{2,1,0:T(8,128)(2,1)} %dinv.1, bf16[128,256]{1,0:T(8,128)(2,1)} %adj.1, bf16[2,128,256]{2,1,0:T(8,128)(2,1)} %side.1, f32[27,4096]{1,0:T(8,128)} %coef_all.1, ...), custom_call_target="tpu_custom_call" | custom-call | flops 1000000000 | bytes 4000000 | tf_op jit(solution)/shard_map/pallas_call | solution.py:437
  80.6 0.0 copy-start
  80.6 1.5 %copy.11 = bf16[4,32,256]{2,1,0:T(8,128)(2,1)} copy(bf16[4,32,256]{2,1,0:T(8,128)(2,1)} %get-tuple-element.8) | data formatting | bytes 131072
  82.1 0.0 copy-done
  82.1 0.5 copy.12
Async XLA Ops:
  80.6 1.5 %copy-start = (f32[1,128]{1,0:T(1,128)S(1)}, f32[1,128]{1,0:T(1,128)}, u32[]{:S(2)}) copy-start(f32[1,128]{1,0:T(1,128)} %get-tuple-element.5) | copy-start | bytes 1540

commit v5 on v4

--- a/solution.py
+++ b/solution.py
@@ -306,7 +306,7 @@
             for d in (4, -4):
                 signal(tick.at[1], z_peer(d))
         if j == 1:
-            for d in range(1, NC):
+            for d in (4, 3, 5, 6, 2, 7, 1):
                 part = pl.ds(pl.multiple_of(c_index(d) * SRC, SRC), SRC)
                 send(s_send.at[part, :], s_got.at[zc], sa_s, sa_r, c_peer(d))
             pl.semaphore_wait(tick.at[1], 2)
@@ -360,6 +360,10 @@
                 whole = (y_full[j, some, :].astype(F32) - total(6 - j, half)).astype(BF16)
             z_some = dot(whole, d_whole(j), NN).astype(BF16)
             z_own[j, some, :] = z_some
+            if j == 0:
+                part = pl.ds(half * HALF, HALF)
+                for d in (2, 1, 3):
+                    send(z_own.at[0, part], z_all.at[0, y, part], za_s.at[0], za_r.at[0], y_peer(d))
             if j > 0:
                 term = dot(z_some, l_whole(j, j - 1), NN)
                 if j - 1 in later_term:
@@ -367,7 +371,7 @@
                 share(7 - j, half, term)
         z_j = z_own[j]
         z_all[j, y] = z_j
-        for d in (2, 1, 3):
+        for d in (2, 1, 3) if j > 0 else ():
             send(z_own.at[j], z_all.at[j, y], za_s.at[j], za_r.at[j], y_peer(d))
         if j > 0:
             for earlier in range(j - 1):

time: 82.8 us -> 82.8 us (level)
  no operation moved by 1% of the time
where the time goes in v5:
time: 82.8 us; the launch traced here: 82.6 us
  Pallas kernels  79.9 us (96%)
  local copies, waits for them, and re-layouts  1.99 us (2%)
    pallas_call x1, Pallas kernels, shards(): pl.pallas_call(kernel, out_shape=(jax.ShapeDtypeStruct((PANELS, PART, 256...  79.9 us
    unnamed x4, local copies, waits for them, and re-layouts  1.99 us

profile of v5, /device:TPU:1, one launch (start us, length us, event | category | flops | bytes accessed | tf_op | source)
XLA Modules:
  0.0 82.6 jit_solution(4334665563850400285)
XLA Ops:
  0.6 79.9 %shard_map.86 = (bf16[4,32,256]{2,1,0:T(8,128)(2,1)}, f32[1,128]{1,0:T(1,128)}) custom-call(bf16[4,32,256]{2,1,0:T(8,128)(2,1)} %rhs.1, bf16[6,32,1024]{2,1,0:T(8,128)(2,1)} %lower.1, bf16[4,32,1024]{2,1,0:T(8,128)(2,1)} %dinv.1, bf16[128,256]{1,0:T(8,128)(2,1)} %adj.1, bf16[2,128,256]{2,1,0:T(8,128)(2,1)} %side.1, f32[27,4096]{1,0:T(8,128)} %coef_all.1, ...), custom_call_target="tpu_custom_call" | custom-call | flops 1000000000 | bytes 4000000 | tf_op jit(solution)/shard_map/pallas_call | solution.py:441
  80.6 0.0 copy-start
  80.6 1.5 %copy.11 = bf16[4,32,256]{2,1,0:T(8,128)(2,1)} copy(bf16[4,32,256]{2,1,0:T(8,128)(2,1)} %get-tuple-element.8) | data formatting | bytes 131072
  82.1 0.0 copy-done
  82.1 0.5 copy.12
Async XLA Ops:
  80.6 1.5 %copy-start = (f32[1,128]{1,0:T(1,128)S(1)}, f32[1,128]{1,0:T(1,128)}, u32[]{:S(2)}) copy-start(f32[1,128]{1,0:T(1,128)} %get-tuple-element.5) | copy-start | bytes 1540
